TPU v7x, 1024 devices: a whole 4x4x32 slice. The times are simulated.
1024 devices in a mesh: dp: 32 (over y, z_lo), expert: 8 (over x, core), tensor: 4 (over z_hi).
Axes of the slice: x: 4, y: 4, z: 32 (z_hi: 4, z_lo: 8; z = z_hi * 8 + z_lo), core: 2. Of those that a mesh axis runs over, the one named last changes fastest.
Arguments:
- tokens: bfloat16 [512, 6144], P('expert', 'tensor'), may hold values from -6 to 6
- expert_ids: int32 [512, 2], P('expert'), may hold values from 0 to 7, all different within a row; in each aligned block of 64 rows (0 to 63, 64 to 127, ...) at most 32 rows name the same one
- w_gate: bfloat16 [8, 6144, 8192], P('expert', 'tensor', 'dp'), may hold values from -0.078125 to 0.078125
- w_up: bfloat16 [8, 6144, 8192], P('expert', 'tensor', 'dp'), may hold values from -0.078125 to 0.078125
- hidden_grad: bfloat16 [8, 256, 8192], P('expert', None, 'dp'), may hold values from -6 to 6
Outputs:
- tokens_grad: bfloat16 [512, 6144], P('expert', 'tensor')
- gate_grad: bfloat16 [8, 6144, 8192], P('expert', 'tensor', 'dp')
- up_grad: bfloat16 [8, 6144, 8192], P('expert', 'tensor', 'dp')
Inputs may be any that keep to these rules, and one draw needn't show every extreme that they name: `expert_ids`: the two ids of a token differ. Within each group of 64 tokens no expert is named by more than 32 tokens.
All inputs are finite; a program needn't handle non-finite values.
Results may differ from a plain program's by a relative error of at most 0.0049.
Values may be sent and summed in bfloat16 or wider, within the bound.
A program may use at most 32 MiB of HBM per device.

v0:
```python
import jax
import jax.numpy as jnp
from jax import lax
from jax.sharding import PartitionSpec as P


def slot_table(expert_ids, expert_count, slot_count):
    flat_ids = expert_ids.reshape(-1)
    labels = jnp.arange(expert_count, dtype=jnp.int32)
    one_hot = (flat_ids[:, None] == labels[None, :]).astype(jnp.int32)
    before = jnp.cumsum(one_hot, axis=0) - one_hot
    slot_rank = jnp.sum(before * one_hot, axis=1)
    target = (flat_ids * slot_count + slot_rank).reshape(expert_ids.shape[0], 2)
    row_index = jnp.arange(expert_count * slot_count, dtype=jnp.int32)
    hits = (row_index[:, None, None] == target[None, :, :]).astype(jnp.int32)
    return jnp.sum(hits, axis=2).astype(jnp.bfloat16)


def combine(placement, returned):
    flat_rows = returned.reshape(placement.shape[0], -1)
    return lax.dot_general(
        placement.astype(jnp.float32),
        flat_rows,
        (((0,), (0,)), ((), ())),
        precision=lax.Precision.HIGHEST,
        preferred_element_type=jnp.float32,
    )


def on_device(tokens, expert_ids, w_gate, w_up, hidden_grad):
    group_count = lax.axis_size("expert")
    local_experts = w_gate.shape[0]
    expert_count = local_experts * group_count
    slot_count = hidden_grad.shape[1] // group_count
    width_local = tokens.shape[1]
    placement = slot_table(expert_ids, expert_count, slot_count)
    outgoing = jnp.dot(placement, tokens, preferred_element_type=jnp.float32).astype(jnp.bfloat16)
    outgoing = outgoing.reshape(group_count, local_experts * slot_count, width_local)
    arrived = lax.all_to_all(outgoing, "expert", split_axis=0, concat_axis=0, tiled=True)
    arrived = arrived.reshape(group_count, local_experts, slot_count, width_local).transpose(
        1, 0, 2, 3
    )
    arrived = arrived.reshape(local_experts, group_count * slot_count, width_local)
    gate_part = jnp.einsum("erd,edf->erf", arrived, w_gate, preferred_element_type=jnp.float32)
    up_part = jnp.einsum("erd,edf->erf", arrived, w_up, preferred_element_type=jnp.float32)
    gate_pre, up_pre = lax.psum((gate_part, up_part), "tensor")
    upstream = hidden_grad.astype(jnp.float32)
    sigmoid_gate = jax.nn.sigmoid(gate_pre)
    d_gate = (upstream * up_pre * sigmoid_gate * (1.0 + gate_pre * (1.0 - sigmoid_gate))).astype(
        jnp.bfloat16
    )
    d_up = (upstream * gate_pre * sigmoid_gate).astype(jnp.bfloat16)
    gate_grad = jnp.einsum(
        "erd,erf->edf", arrived, d_gate, preferred_element_type=jnp.float32
    ).astype(jnp.bfloat16)
    up_grad = jnp.einsum("erd,erf->edf", arrived, d_up, preferred_element_type=jnp.float32).astype(
        jnp.bfloat16
    )
    partial_rows = jnp.einsum("erf,edf->erd", d_gate, w_gate, preferred_element_type=jnp.float32)
    partial_rows = partial_rows + jnp.einsum(
        "erf,edf->erd", d_up, w_up, preferred_element_type=jnp.float32
    )
    summed = lax.psum(partial_rows, "dp")
    split_rows = summed.reshape(local_experts, group_count, slot_count, width_local).transpose(
        1, 0, 2, 3
    )
    returned = lax.all_to_all(
        split_rows.reshape(group_count, local_experts * slot_count, width_local),
        "expert",
        split_axis=0,
        concat_axis=0,
        tiled=True,
    )
    result = combine(placement, returned)
    return (result.astype(jnp.bfloat16), gate_grad, up_grad)


def solution(mesh):
    in_specs = (
        P("expert", "tensor"),
        P("expert", None),
        P("expert", "tensor", "dp"),
        P("expert", "tensor", "dp"),
        P("expert", None, "dp"),
    )
    out_specs = (P("expert", "tensor"), P("expert", "tensor", "dp"), P("expert", "tensor", "dp"))
    return jax.shard_map(
        on_device, mesh=mesh, in_specs=in_specs, out_specs=out_specs, check_vma=False
    )
```

profile of v0, /device:TPU:1, one launch (start us, length us, event | category | flops | bytes accessed | tf_op | source)
XLA Modules:
  0.0 695.4 jit_solution(15863243480402243906)
XLA Ops:
  7.2 0.0 copy-start
  7.2 0.0 all-reduce.6.cloned.1.call-start
  7.2 0.8 copy.18
  8.1 0.1 eq.29
  8.2 0.1 fusion.16
  8.3 0.2 reduce_window_sum.11
  8.5 0.2 select_reduce_fusion
  8.6 0.1 reduce_sum.21
  8.8 0.1 copy.19
  8.9 0.7 multiply_add_fusion
  9.6 0.1 convert_reduce_fusion
  9.7 0.0 copy-start.3
  9.7 1.3 convolution_convert_fusion.2
  11.0 0.0 copy-done.3
  11.0 0.0 copy-start.1
  11.0 28.9 %all_to_all.10 = bf16[8,32,1536]{2,1,0:T(8,128)(2,1)S(1)} all-to-all(bf16[8,32,1536]{2,1,0:T(8,128)(2,1)S(1)} %bitcast.44), channel_id=1, replica_groups=mesh['dp'=32,'expert'=8,'tensor'=4] {'expert'}, dimensions={0} | all-to-all | bytes 1572864 | tf_op jit(solution)/shard_map/all_to_all | solution.py:39
  39.9 0.0 copy-done
  39.9 1.1 convolution_bitcast_fusion
  41.0 0.0 copy-done.1
  41.0 0.0 copy-start.5
  41.0 1.1 convolution_bitcast_fusion.1
  42.1 0.0 all-reduce.6.cloned.1.call-update
  42.1 0.0 all-reduce.4.cloned.1.call-start
  42.2 144.4 %all-reduce.6.cloned.1.call-done = (f32[1,256,256]{2,1,0:T(8,128)}, f32[1,256,256]{2,1,0:T(8,128)}) async-done(((f32[1,256,256]{2,1,0:T(8,128)}, f32[1,256,256]{2,1,0:T(8,128)}), (f32[1,256,256]{2,1,0:T(8,128)}, f32[1,256,256]{2,1,0:T(8,128)})) %all-reduce.6.cloned.1.call-update) | async-done | bytes 524304 | tf_op jit(solution)/shard_map/psum | solution.py:46
  186.6 0.0 copy-done.5
  186.6 0.0 copy-start.2
  186.6 1.2 fusion.9
  187.7 0.4 fusion.2
  188.2 0.0 copy-done.2
  188.2 1.6 convolution_add_fusion
  189.7 0.0 all-reduce.4.cloned.1.call-update
  189.8 450.5 %all-reduce.4.cloned.1.call-done = f32[8,32,1536]{2,1,0:T(8,128)} async-done(((f32[8,32,1536]{2,1,0:T(8,128)}), f32[8,32,1536]{2,1,0:T(8,128)}) %all-reduce.4.cloned.1.call-update) | async-done | bytes 1572880 | tf_op jit(solution)/shard_map/psum | solution.py:63
  640.3 26.1 %all-to-all-start.1 = ((f32[8,32,1536]{2,1,0:T(8,128)}), f32[8,32,1536]{2,1,0:T(8,128)S(1)}, u32[]{:S(2)}, u32[]{:S(2)}) async-start(f32[8,32,1536]{2,1,0:T(8,128)} %all-reduce.4.cloned.1.call-done), calls=%async_computation.1 | async-start | bytes 3145728 | tf_op jit(solution)/shard_map/all_to_all | solution.py:67
  666.4 0.0 copy-start.6
  666.4 1.3 fusion
  667.7 0.0 copy-done.6
  667.7 0.0 copy-start.4
  667.7 1.3 fusion.1
  669.0 18.1 %all-to-all-done.1 = f32[8,32,1536]{2,1,0:T(8,128)S(1)} async-done(((f32[8,32,1536]{2,1,0:T(8,128)}), f32[8,32,1536]{2,1,0:T(8,128)S(1)}, u32[]{:S(2)}, u32[]{:S(2)}) %all-to-all-start.1) | async-done | bytes 1572896 | tf_op jit(solution)/shard_map/all_to_all | solution.py:67
  687.1 0.0 copy-done.4
  687.1 1.4 convolution_convert_fusion.3
Async XLA Ops:
  7.2 32.8 %copy-start = (bf16[1,1536,256]{2,1,0:T(8,128)(2,1)S(1)}, bf16[1,1536,256]{2,1,0:T(8,128)(2,1)}, u32[]{:S(2)}) copy-start(bf16[1,1536,256]{2,1,0:T(8,128)(2,1)} %param.7) | copy-start | bytes 2359300
  7.2 179.4 %all-reduce.6.cloned.1.call-start = ((), (), s32[]{:S(2)}) async-start(), calls=%async_computation.3 | async-start | bytes 1048576 | tf_op jit(solution)/shard_map/psum | solution.py:46
  9.7 1.4 copy-start.3
  11.0 30.0 %copy-start.1 = (bf16[1,1536,256]{2,1,0:T(8,128)(2,1)S(1)}, bf16[1,1536,256]{2,1,0:T(8,128)(2,1)}, u32[]{:S(2)}) copy-start(bf16[1,1536,256]{2,1,0:T(8,128)(2,1)} %param.8) | copy-start | bytes 2359300
  41.0 145.5 %copy-start.5 = (bf16[1,256,256]{2,1,0:T(8,128)(2,1)S(1)}, bf16[1,256,256]{2,1,0:T(8,128)(2,1)}, u32[]{:S(2)}) copy-start(bf16[1,256,256]{2,1,0:T(8,128)(2,1)} %param.9) | copy-start | bytes 393220
  42.1 598.2 %all-reduce.4.cloned.1.call-start = ((), (), s32[]{:S(2)}) async-start(), calls=%async_computation.2 | async-start | bytes 3145728 | tf_op jit(solution)/shard_map/psum | solution.py:63
  186.6 1.6 copy-start.2
  640.3 46.8 %all-to-all-start.1 = ((f32[8,32,1536]{2,1,0:T(8,128)}), f32[8,32,1536]{2,1,0:T(8,128)S(1)}, u32[]{:S(2)}, u32[]{:S(2)}) async-start(f32[8,32,1536]{2,1,0:T(8,128)} %all-reduce.4.cloned.1.call-done), calls=%async_computation.1 | async-start | bytes 3145728 | tf_op jit(solution)/shard_map/all_to_all | solution.py:67
  666.4 1.3 copy-start.6
  667.7 19.4 %copy-start.4 = (s32[256,64]{0,1:T(8,128)S(1)}, s32[256,64]{0,1:T(8,128)}, u32[]{:S(2)}) copy-start(s32[256,64]{0,1:T(8,128)} %copy-done.3) | copy-start | bytes 196612
Sparse Core Ops, SparseCore 0:
  42.2 144.2 all-reduce.5
  190.1 450.2 all-reduce.3
where the time goes:
time: 696 us; the launch traced here: 695 us
  waiting for transfers between devices  613 us (88%)
  blocking collectives  28.9 us (4%)
  starting transfers between devices  26.1 us (4%)
  between operations  14.1 us (2%)
  matrix products  9.5 us (1%)
    psum x1, waiting for transfers between devices, on_device(): summed = lax.psum(partial_rows, 'dp')  451 us
    psum x1, waiting for transfers between devices, on_device(): gate_pre, up_pre = lax.psum((gate_part, up_part), 'tensor')  144 us
    all_to_all x1, blocking collectives, on_device(): lax.all_to_all(outgoing, 'expert', split_axis=0, concat_axis=0, tiled=True)  28.9 us
    all_to_all x1, starting transfers between devices, on_device(): lax.all_to_all(split_rows.reshape(group_count, local_experts * slot_count...  26.1 us
    all_to_all x1, waiting for transfers between devices, on_device(): lax.all_to_all(split_rows.reshape(group_count, local_experts * slot_count...  18.1 us
  transfers between devices with their start and end apart: 3, of which 3 were waited for; matrix products, arithmetic and copies ran while one was open for 0% of the time, Pallas kernels for 0%

commit v1 on v0

v1 whole, which is shorter than its diff:
```python
import functools

import jax
import jax.numpy as jnp
from jax import lax
from jax.experimental import pallas as pl
from jax.experimental.pallas import tpu as pltpu
from jax.sharding import PartitionSpec as P

MESH = pl.DeviceIdType.MESH
F32, BF16 = jnp.float32, jnp.bfloat16
ANY = pl.ANY
VMEM = pltpu.VMEM
DMA = pltpu.SemaphoreType.DMA

SLABS = {
    4: ((0, 0), (0, 1), (2, 0), (2, 1), (1, 0), (3, 0), (1, 1), (3, 1)),
    1: ((0, 0), (0, 1)),
}


def remote(src, dst, send, recv, device):
    return pltpu.make_async_remote_copy(
        src_ref=src, dst_ref=dst, send_sem=send, recv_sem=recv, device_id=device, device_id_type=MESH
    )


def kernel(
    sizes,
    ids_ref,
    tok_ref,
    hg_hbm,
    wg_hbm,
    wu_hbm,
    tg_out,
    gg_hbm,
    ug_hbm,
    w_ref,
    hg_ref,
    out_ref,
    x_ref,
    p_ref,
    d_ref,
    r_ref,
    ret_ref,
    s1_snd,
    s1_rcv,
    s2_snd,
    s2_rcv,
    sum_ref,
    ysnd,
    yrcv,
    acc_ref,
    zsnd,
    zrcv,
    og_ref,
    gg_ref,
    ug_ref,
    load_sem,
    store_sem,
    a_send,
    a_recv,
    s1_send,
    s1_recv,
    s2_send,
    s2_recv,
    g1_send,
    g1_recv,
    g2_send,
    g2_recv,
    r_send,
    r_recv,
    y_send,
    y_recv,
    z_send,
    z_recv,
    h_send,
    h_recv,
    o_send,
    o_recv,
):
    ny, nz, nx = sizes
    experts = 2 * nx
    tokens, width = tok_ref.shape
    slots = r_ref.shape[0] // experts
    half = w_ref.shape[1] // 2
    slabs = SLABS[nx]
    chunks = len(slabs) // 2
    rows = 2 * slots
    part = rows // 4

    expert = lax.axis_index("expert")
    core = expert % 2
    x = expert // 2
    dp = lax.axis_index("dp")
    y, zl = dp // nz, dp % nz
    zh = lax.axis_index("tensor")
    up, down = {"tensor": (zh + 1) % 4}, {"tensor": (zh + 3) % 4}

    def place(dx, c):
        return {0: c, 2: 2 + c, 1: 4 + 2 * c, 3: 5 + 2 * c}[dx]

    loads = [
        pltpu.make_async_copy(wg_hbm, w_ref.at[:, pl.ds(0, half)], load_sem.at[0]),
        pltpu.make_async_copy(wu_hbm, w_ref.at[:, pl.ds(half, half)], load_sem.at[1]),
        pltpu.make_async_copy(hg_hbm, hg_ref, load_sem.at[2]),
    ]
    for load in loads:
        load.start()

    barrier = pltpu.get_barrier_semaphore()
    greeted = 0
    for k in range(1, experts):
        pl.semaphore_signal(barrier, 1, device_id={"expert": (expert + k) % experts}, device_id_type=MESH)
        greeted += 1
    for peer in (up, down):
        pl.semaphore_signal(barrier, 1, device_id=peer, device_id_type=MESH)
        greeted += 1
    for k in range(1, ny):
        pl.semaphore_signal(barrier, 1, device_id={"dp": (y + k) % ny * nz + zl}, device_id_type=MESH)
        greeted += 1
    for k in range(1, nz):
        pl.semaphore_signal(barrier, 1, device_id={"dp": y * nz + (zl + k) % nz}, device_id_type=MESH)
        greeted += 1

    total = experts * slots
    lane = lax.broadcasted_iota(jnp.int32, (tokens, total), 1)
    e_of, c_of = lane // slots, lane % slots
    chosen = (ids_ref[:, 0:1] == e_of) | (ids_ref[:, 1:2] == e_of)
    earlier = lax.broadcasted_iota(jnp.int32, (tokens, tokens), 0) > lax.broadcasted_iota(
        jnp.int32, (tokens, tokens), 1
    )
    before = jnp.dot(
        jnp.where(earlier, 1.0, 0.0).astype(BF16),
        jnp.where(chosen, 1.0, 0.0).astype(BF16),
        preferred_element_type=F32,
    )
    table = jnp.where(chosen & (before == c_of.astype(F32)), 1.0, 0.0).astype(BF16)
    out_ref[...] = lax.dot_general(
        table, tok_ref[...], (((0,), (0,)), ((), ())), preferred_element_type=F32
    ).astype(BF16)

    pl.semaphore_wait(barrier, greeted)

    def block(e):
        return pl.ds(pl.multiple_of(e * slots, slots), slots)

    sends = []
    dxs = [0, 1, 3, 2] if nx == 4 else [0]
    flat = 0
    for dx in dxs:
        for c in range(2):
            if dx == 0 and c == 1:
                continue
            other = 1 - core if dx == 0 else c
            to = ((x + nx - dx) % nx) * 2 + other
            slab = place(dx, core)
            copy = remote(
                out_ref.at[block(to)], x_ref.at[block(slab)], a_send.at[flat], a_recv.at[slab], {"expert": to}
            )
            copy.start()
            sends.append(copy)
            flat += 1
    x_ref[block(core), :] = out_ref[block(expert), :]

    def source(p):
        dx, c = slabs[p]
        return ((x + dx) % nx) * 2 + c

    def wait_slabs(j):
        for p in (2 * j, 2 * j + 1):
            if slabs[p][0] == 0:
                if p == 0:
                    q = 1 - core
                    remote(
                        out_ref.at[block(0)], x_ref.at[block(q)], a_send.at[0], a_recv.at[q], {"expert": expert}
                    ).wait_recv()
            else:
                remote(
                    out_ref.at[block(0)], x_ref.at[block(p)], a_send.at[0], a_recv.at[p], {"expert": expert}
                ).wait_recv()

    def piece(j, k):
        return pl.ds(pl.multiple_of(j * rows + k * part, part), part)

    lo, hi = pl.ds(0, half), pl.ds(half, half)
    dirs = ((up, lo), (down, hi))

    def s1(j, d):
        return remote(s1_snd.at[j, d], s1_rcv.at[j, d], s1_send.at[j, d], s1_recv.at[j, d], dirs[d][0])

    def s2(j, d):
        return remote(s2_snd.at[j, d], s2_rcv.at[j, d], s2_send.at[j, d], s2_recv.at[j, d], dirs[d][0])

    def g1(j, d):
        ref = d_ref.at[piece(j, zh)]
        return remote(ref, ref, g1_send.at[j, d], g1_recv.at[j, d], dirs[d][0])

    def g2(j, d):
        ref = d_ref.at[piece(j, (zh + (3 if d == 0 else 1)) % 4), dirs[d][1]]
        return remote(ref, ref, g2_send.at[j, d], g2_recv.at[j, d], dirs[d][0])

    def stage0(j):
        wait_slabs(j)
        if j == 0:
            loads[0].wait()
            loads[1].wait()
        own = pl.ds(j * rows, rows)
        p_ref[own, :] = jnp.dot(x_ref[own, :], w_ref[...], preferred_element_type=F32)
        far = piece(j, (zh + 2) % 4)
        s1_snd[j, 0] = p_ref[far, lo].astype(BF16)
        s1_snd[j, 1] = p_ref[far, hi].astype(BF16)
        for d in range(2):
            s1(j, d).start()
            sends.append(s1(j, d))

    def stage1(j):
        for d in range(2):
            to = piece(j, (zh + (1 if d == 0 else 3)) % 4)
            mixed, plain = (lo, hi) if d == 0 else (hi, lo)
            s2_snd[j, d, :, plain] = p_ref[to, plain].astype(BF16)
            s1(j, d).wait_recv()
            s2_snd[j, d, :, mixed] = (p_ref[to, mixed] + s1_rcv[j, d].astype(F32)).astype(BF16)
            s2(j, d).start()
            sends.append(s2(j, d))

    def stage2(j):
        if j == 0:
            loads[2].wait()
        mine = piece(j, zh)
        group = jnp.where(zh < 2, source(2 * j), source(2 * j + 1))
        hg_rows = pl.ds(pl.multiple_of(group * slots + zh % 2 * part, part), part)
        upstream = hg_ref[hg_rows, :].astype(F32)
        for d in range(2):
            s2(j, d).wait_recv()
        gate = p_ref[mine, lo] + s2_rcv[j, 0, :, lo].astype(F32) + s2_rcv[j, 1, :, lo].astype(F32)
        upp = p_ref[mine, hi] + s2_rcv[j, 0, :, hi].astype(F32) + s2_rcv[j, 1, :, hi].astype(F32)
        sg = jax.nn.sigmoid(gate)
        d_ref[mine, lo] = (upstream * upp * sg * (1.0 + gate * (1.0 - sg))).astype(BF16)
        d_ref[mine, hi] = (upstream * gate * sg).astype(BF16)
        for d in range(2):
            g1(j, d).start()
            sends.append(g1(j, d))

    def got1(j, d):
        ref = d_ref.at[piece(j, (zh + (3 if d == 0 else 1)) % 4)]
        return remote(ref, ref, g1_send.at[j, d], g1_recv.at[j, d], dirs[d][0])

    def got2(j, d):
        ref = d_ref.at[piece(j, (zh + 2) % 4), dirs[d][1]]
        return remote(ref, ref, g2_send.at[j, d], g2_recv.at[j, d], dirs[d][0])

    def stage3(j):
        for d in range(2):
            got1(j, d).wait_recv()
            g2(j, d).start()
            sends.append(g2(j, d))

    def stage4(j):
        for d in range(2):
            got2(j, d).wait_recv()
        own = pl.ds(j * rows, rows)
        r_ref[own, :] = lax.dot_general(
            d_ref[own, :], w_ref[...], (((1,), (1,)), ((), ())), preferred_element_type=F32
        ).astype(BF16)
        for p in (2 * j, 2 * j + 1):
            dx, c = slabs[p]
            if dx == 0:
                if p % 2:
                    continue
                p, to = 1 - core, x * 2 + 1 - core
            else:
                to = source(p)
            index = place((nx - dx) % nx, core)
            copy = remote(
                r_ref.at[block(p)], ret_ref.at[block(expert)], r_send.at[p], r_recv.at[index], {"expert": to}
            )
            copy.start()
            sends.append(copy)
        if j == 0:
            ret_ref[block(expert), :] = r_ref[block(core), :]

    stages = (stage0, stage1, stage2, stage3, stage4)
    for t in range(chunks + len(stages) - 1):
        for s in reversed(range(len(stages))):
            if 0 <= t - s < chunks:
                stages[s](t - s)

    step = min(256, width)

    def grads(i, carry):
        cols = pl.ds(pl.multiple_of(i * step, step), step)
        both = lax.dot_general(
            x_ref[:, cols], d_ref[...], (((0,), (0,)), ((), ())), preferred_element_type=F32
        ).astype(BF16)
        gg_ref[cols, :] = both[:, :half]
        ug_ref[cols, :] = both[:, half:]
        return carry

    lax.fori_loop(0, width // step, grads, 0)
    stores = [
        pltpu.make_async_copy(gg_ref, gg_hbm, store_sem.at[0]),
        pltpu.make_async_copy(ug_ref, ug_hbm, store_sem.at[1]),
    ]
    for store in stores:
        store.start()

    for p in range(len(slabs)):
        dx, c = slabs[p]
        if dx == 0:
            if p:
                continue
            index, e = 1 - core, x * 2 + 1 - core
        else:
            index, e = p, source(p)
        remote(
            r_ref.at[block(0)], ret_ref.at[block(e)], r_send.at[0], r_recv.at[index], {"expert": expert}
        ).wait_recv()
    sum_ref[...] = jnp.dot(table, ret_ref[...], preferred_element_type=F32)

    share = tokens // ny

    def band(k):
        return pl.ds(pl.multiple_of(k * share, share), share)

    mine = band(y)
    acc = sum_ref[mine, :]
    if ny > 1:
        ysnd[...] = sum_ref[...].astype(BF16)
        for k in range(1, ny):
            to = (y + k) % ny
            copy = remote(
                ysnd.at[band(to)], yrcv.at[k - 1], y_send.at[k - 1], y_recv.at[k - 1], {"dp": to * nz + zl}
            )
            copy.start()
            sends.append(copy)
        for k in range(1, ny):
            remote(
                ysnd.at[band(0)], yrcv.at[k - 1], y_send.at[k - 1], y_recv.at[k - 1], {"dp": dp}
            ).wait_recv()
            acc = acc + yrcv[k - 1].astype(F32)
    acc_ref[...] = acc

    owners = min(4, nz)
    first = (nz - owners) // 2
    wide = width // owners
    zsnd[...] = acc.astype(BF16)

    def z_out(m):
        rel = (zl + nz - (first + m)) % nz
        return remote(
            zsnd.at[:, pl.ds(m * wide, wide)],
            zrcv.at[rel],
            z_send.at[m],
            z_recv.at[rel],
            {"dp": y * nz + first + m},
        )

    is_owner = (zl >= first) & (zl < first + owners)
    my_cols = pl.ds(pl.multiple_of(jnp.clip(zl - first, 0, owners - 1) * wide, 128), wide)
    my_m = jnp.clip(zl - first, 0, owners - 1)

    def h_out(k):
        ref = og_ref.at[mine, my_cols]
        return remote(ref, ref, h_send.at[k], h_recv.at[my_m], {"dp": y * nz + (zl + k) % nz})

    for m in range(owners):
        pl.when(zl != first + m)(lambda m=m: z_out(m).start())

    @pl.when(is_owner)
    def _():
        value = acc_ref[:, my_cols]
        for k in range(1, nz):
            remote(
                zsnd.at[:, pl.ds(0, wide)], zrcv.at[k], z_send.at[0], z_recv.at[k], {"dp": dp}
            ).wait_recv()
            value = value + zrcv[k].astype(F32)
        og_ref[mine, my_cols] = value.astype(BF16)
        for k in range(1, nz):
            h_out(k).start()

    for m in range(owners):

        @pl.when(zl != first + m)
        def _(m=m):
            ref = og_ref.at[mine, pl.ds(m * wide, wide)]
            remote(ref, ref, h_send.at[0], h_recv.at[m], {"dp": dp}).wait_recv()

    for k in range(1, ny):
        ref = og_ref.at[mine]
        copy = remote(ref, ref, o_send.at[k - 1], o_recv.at[k - 1], {"dp": (y + k) % ny * nz + zl})
        copy.start()
        sends.append(copy)
    for k in range(1, ny):
        ref = og_ref.at[band((y + ny - k) % ny)]
        remote(ref, ref, o_send.at[k - 1], o_recv.at[k - 1], {"dp": dp}).wait_recv()
    tg_out[...] = og_ref[...]

    for copy in sends:
        copy.wait_send()
    for m in range(owners):
        pl.when(zl != first + m)(lambda m=m: z_out(m).wait_send())

    @pl.when(is_owner)
    def _():
        for k in range(1, nz):
            h_out(k).wait_send()

    for store in stores:
        store.wait()


def on_device(sizes, tokens, expert_ids, w_gate, w_up, hidden_grad):
    ny, nz, nx = sizes
    count, width = tokens.shape
    half = w_gate.shape[2]
    rows = hidden_grad.shape[1]
    chunks = nx
    part = rows // chunks // 4
    share = count // ny
    owners = min(4, nz)
    near = max(ny - 1, 1)
    scratch = [
        VMEM((width, 2 * half), BF16),
        VMEM((rows, half), BF16),
        VMEM((rows, width), BF16),
        VMEM((rows, width), BF16),
        VMEM((rows, 2 * half), F32),
        VMEM((rows, 2 * half), BF16),
        VMEM((rows, width), BF16),
        VMEM((rows, width), BF16),
        VMEM((chunks, 2, part, half), BF16),
        VMEM((chunks, 2, part, half), BF16),
        VMEM((chunks, 2, part, 2 * half), BF16),
        VMEM((chunks, 2, part, 2 * half), BF16),
        VMEM((count, width), F32),
        VMEM((count, width), BF16),
        VMEM((near, share, width), BF16),
        VMEM((share, width), F32),
        VMEM((share, width), BF16),
        VMEM((nz, share, width // owners), BF16),
        VMEM((count, width), BF16),
        VMEM((width, half), BF16),
        VMEM((width, half), BF16),
        DMA((3,)),
        DMA((2,)),
        DMA((2 * nx,)),
        DMA((2 * nx,)),
    ]
    scratch += [DMA((chunks, 2)) for _ in range(8)]
    scratch += [
        DMA((2 * nx,)),
        DMA((2 * nx,)),
        DMA((near,)),
        DMA((near,)),
        DMA((owners,)),
        DMA((nz,)),
        DMA((nz,)),
        DMA((owners,)),
        DMA((near,)),
        DMA((near,)),
    ]
    vmem = pl.BlockSpec(memory_space=VMEM)
    hbm = pl.BlockSpec(memory_space=ANY)
    tokens_grad, gate_grad, up_grad = pl.pallas_call(
        functools.partial(kernel, sizes),
        out_shape=(
            jax.ShapeDtypeStruct((count, width), BF16),
            jax.ShapeDtypeStruct((width, half), BF16),
            jax.ShapeDtypeStruct((width, half), BF16),
        ),
        in_specs=[vmem, vmem, hbm, hbm, hbm],
        out_specs=(vmem, hbm, hbm),
        scratch_shapes=scratch,
        compiler_params=pltpu.CompilerParams(
            collective_id=0, has_side_effects=True, vmem_limit_bytes=40 * 1024 * 1024
        ),
    )(expert_ids, tokens, hidden_grad[0], w_gate[0], w_up[0])
    return tokens_grad, gate_grad[None], up_grad[None]


def solution(mesh):
    dp, experts = mesh.shape["dp"], mesh.shape["expert"]
    sizes = {32: (4, 8), 4: (2, 2), 1: (1, 1)}[dp] + (experts // 2,)
    in_specs = (
        P("expert", "tensor"),
        P("expert", None),
        P("expert", "tensor", "dp"),
        P("expert", "tensor", "dp"),
        P("expert", None, "dp"),
    )
    out_specs = (P("expert", "tensor"), P("expert", "tensor", "dp"), P("expert", "tensor", "dp"))
    return jax.shard_map(
        functools.partial(on_device, sizes),
        mesh=mesh,
        in_specs=in_specs,
        out_specs=out_specs,
        check_vma=False,
    )
```

time: 696 us -> 126 us (0.18)
  waiting for transfers between devices: 613 us -> 0 us
  Pallas kernels: 0 us -> 118 us
  blocking collectives: 28.9 us -> 0 us
  starting transfers between devices: 26.1 us -> 0 us
  between operations: 14.1 us -> 0.65 us
  matrix products: 9.5 us -> 0 us
    psum x2 -> x0, waiting for transfers between devices: 595 us -> none  [the longest x1 451 us: on_device(): summed = lax.psum(partial_rows, 'dp')]
    pallas_call x0 -> x1, Pallas kernels: none -> 118 us  [on_device(): pl.pallas_call(functools.partial(kernel, sizes), out_shape=(jax.ShapeDtyp...]
    all_to_all x1 -> x0, blocking collectives: 28.9 us -> none  [on_device(): lax.all_to_all(outgoing, 'expert', split_axis=0, concat_axis=0, tiled=True)]
    all_to_all x1 -> x0, starting transfers between devices: 26.1 us -> none  [on_device(): lax.all_to_all(split_rows.reshape(group_count, local_experts * slot_count...]
    all_to_all x1 -> x0, waiting for transfers between devices: 18.1 us -> none  [on_device(): lax.all_to_all(split_rows.reshape(group_count, local_experts * slot_count...]
    dot_general x8 -> x0, matrix products: 9.5 us -> none  [the longest x1 1.57 us: on_device(): jnp.einsum('erf,edf->erd', d_up, w_up, preferred_element_type=jnp.float32)]
  transfers between devices with their start and end apart: 3 -> 0, of which waited for: 3 -> 0; matrix products, arithmetic and copies ran while one was open for 0% -> 0% of each run, Pallas kernels for 0% -> 0%
where the time goes in v1:
time: 126 us; the launch traced here: 125 us
  Pallas kernels  118 us (94%)
  local copies, waits for them, and re-layouts  7.3 us (6%)
    pallas_call x1, Pallas kernels, on_device(): pl.pallas_call(functools.partial(kernel, sizes), out_shape=(jax.ShapeDtyp...  118 us
    unnamed x14, local copies, waits for them, and re-layouts  7.3 us

profile of v1, /device:TPU:1, one launch (start us, length us, event | category | flops | bytes accessed | tf_op | source)
XLA Modules:
  0.0 125.5 jit_solution(8687252811545019425)
XLA Ops:
  0.6 0.0 copy-start.4
  0.6 0.7 copy-done.4
  1.3 0.1 copy.8.ids_ref
  1.4 0.0 copy-start
  1.4 1.1 copy-done
  2.5 0.0 copy-start.1
  2.5 1.1 copy-done.1
  3.7 0.0 copy-start.2
  3.7 0.9 copy-done.2
  4.6 0.0 copy-start.3
  4.6 0.9 copy-done.3
  5.5 117.5 %shard_map.76 = (bf16[64,1536]{1,0:T(8,128)(2,1)S(1)}, bf16[1536,256]{1,0:T(8,128)(2,1)S(1)}, bf16[1536,256]{1,0:T(8,128)(2,1)S(1)}) custom-call(s32[64,2]{1,0:T(8,128)S(1)} %copy.8.ids_ref, bf16[64,1536]{1,0:T(8,128)(2,1)S(1)} %copy-done.2, bf16[256,256]{1,0:T(8,128)(2,1)S(1)} %bitcast.9, bf16[1536,256]{1,0:T(8,128)(2,1)S(1)} %bitcast.7, ...), custom_call_target="tpu_custom_call" | custom-call | tf_op jit(solution)/shard_map/pallas_call | solution.py:465
  123.0 0.7 copy.12
  123.7 0.9 copy.13
  124.6 0.9 copy.14
Async XLA Ops:
  0.6 0.7 copy-start.4
  1.4 1.1 copy-start
  2.5 1.1 copy-start.1
  3.7 0.9 copy-start.2
  4.6 0.9 copy-start.3

commit v2 on v1

v2 whole, which is shorter than its diff:
```python
import functools

import jax
import jax.numpy as jnp
from jax import lax
from jax.experimental import pallas as pl
from jax.experimental.pallas import tpu as pltpu
from jax.sharding import PartitionSpec as P

MESH = pl.DeviceIdType.MESH
F32, BF16 = jnp.float32, jnp.bfloat16
ANY = pl.ANY
VMEM = pltpu.VMEM
DMA = pltpu.SemaphoreType.DMA

SLABS = {
    4: ((0, 0), (0, 1), (1, 0), (3, 1), (2, 0), (2, 1), (1, 1), (3, 0)),
    1: ((0, 0), (0, 1)),
}


def remote(src, dst, send, recv, device):
    return pltpu.make_async_remote_copy(
        src_ref=src, dst_ref=dst, send_sem=send, recv_sem=recv, device_id=device, device_id_type=MESH
    )


def kernel(
    sizes,
    ids_ref,
    tok_ref,
    hg_hbm,
    wg_hbm,
    wu_hbm,
    tg_out,
    gg_hbm,
    ug_hbm,
    table_ref,
    w_ref,
    hg_ref,
    out_ref,
    x_ref,
    p_ref,
    d_ref,
    r_ref,
    rf_ref,
    yrcv,
    ysum,
    ret_ref,
    s1_snd,
    s1_rcv,
    s2_snd,
    s2_rcv,
    sum_ref,
    zsnd,
    zrcv,
    og_ref,
    gg_ref,
    ug_ref,
    load_sem,
    store_sem,
    a_send,
    a_recv,
    f_send,
    f_recv,
    s1_send,
    s1_recv,
    s2_send,
    s2_recv,
    g1_send,
    g1_recv,
    r_send,
    r_recv,
    y_send,
    y_recv,
    z_send,
    z_recv,
    h_send,
    h_recv,
    o_send,
    o_recv,
):
    ny, nz, nx = sizes
    experts = 2 * nx
    tokens, width = tok_ref.shape
    slots = r_ref.shape[0] // experts
    half = w_ref.shape[1] // 2
    slabs = SLABS[nx]
    cuts = z_send.shape[1]
    share = width // ny
    span = share // cuts
    chunks = len(slabs) // 2
    rows = 2 * slots
    part = rows // 4

    expert = lax.axis_index("expert")
    core = expert % 2
    x = expert // 2
    dp = lax.axis_index("dp")
    y, zl = dp // nz, dp % nz
    zh = lax.axis_index("tensor")
    pair = ({"tensor": zh + 1 - 2 * (zh % 2)}, {"tensor": 3 - zh})
    kept = ((zh + 1) % 4 // 2, zh // 2)

    def place(dx, c):
        return {0: c, 1: 2 + 4 * c, 2: 4 + c, 3: 7 - 4 * c}[dx]

    def cols_of(k):
        return pl.ds(pl.multiple_of(k * share, 128), share)

    def cut_of(k, q):
        return pl.ds(pl.multiple_of(k * share + q * span, 128), span)

    barrier = pltpu.get_barrier_semaphore()
    greeted = 0
    for peer in pair:
        pl.semaphore_signal(barrier, 1, device_id=peer, device_id_type=MESH)
        greeted += 1
    for k in range(1, experts):
        pl.semaphore_signal(barrier, 1, device_id={"expert": (expert + k) % experts}, device_id_type=MESH)
        greeted += 1
    for k in range(1, ny):
        pl.semaphore_signal(barrier, 1, device_id={"dp": (y + k) % ny * nz + zl}, device_id_type=MESH)
        greeted += 1
    for k in range(1, nz):
        pl.semaphore_signal(barrier, 1, device_id={"dp": y * nz + (zl + k) % nz}, device_id_type=MESH)
        greeted += 1

    loads = [
        pltpu.make_async_copy(wg_hbm, w_ref.at[:, pl.ds(0, half)], load_sem.at[0]),
        pltpu.make_async_copy(wu_hbm, w_ref.at[:, pl.ds(half, half)], load_sem.at[1]),
        pltpu.make_async_copy(hg_hbm, hg_ref, load_sem.at[2]),
    ]
    for load in loads:
        load.start()

    total = experts * slots
    row = lax.broadcasted_iota(jnp.int32, (total, tokens), 0)
    chosen = (ids_ref[0:1, :] == row // slots) | (ids_ref[1:2, :] == row // slots)
    earlier = lax.broadcasted_iota(jnp.int32, (tokens, tokens), 0) < lax.broadcasted_iota(
        jnp.int32, (tokens, tokens), 1
    )
    before = jnp.dot(
        jnp.where(chosen, 1.0, 0.0).astype(BF16),
        jnp.where(earlier, 1.0, 0.0).astype(BF16),
        preferred_element_type=F32,
    )
    table = jnp.where(chosen & (before == (row % slots).astype(F32)), 1.0, 0.0)
    table_ref[...] = table.T.astype(BF16)
    out_ref[...] = jnp.dot(table.astype(BF16), tok_ref[...], preferred_element_type=F32).astype(BF16)

    pl.semaphore_wait(barrier, greeted)

    def block(e):
        return pl.ds(pl.multiple_of(e * slots, slots), slots)

    sends = []
    dxs = [0, 2, 1, 3] if nx == 4 else [0]
    flat = 0
    for dx in dxs:
        for c in range(2):
            if dx == 0 and c == 1:
                continue
            other = 1 - core if dx == 0 else c
            to = ((x + nx - dx) % nx) * 2 + other
            slab = place(dx, core)
            src, dst = out_ref.at[block(to)], x_ref.at[block(slab)]
            if dx == 2:
                src, dst = out_ref.at[block(to), cols_of(y)], x_ref.at[block(slab), cols_of(y)]
            copy = remote(src, dst, a_send.at[flat], a_recv.at[slab], {"expert": to})
            copy.start()
            sends.append(copy)
            flat += 1
    x_ref[block(core), :] = out_ref[block(expert), :]

    def source(p):
        dx, c = slabs[p]
        return ((x + dx) % nx) * 2 + c

    def wait_slabs(j):
        for p in (2 * j, 2 * j + 1):
            if slabs[p][0] == 0:
                if p == 0:
                    q = 1 - core
                    remote(
                        out_ref.at[block(0)], x_ref.at[block(q)], a_send.at[0], a_recv.at[q], {"expert": expert}
                    ).wait_recv()
            elif slabs[p][0] != 2:
                remote(
                    out_ref.at[block(0)], x_ref.at[block(p)], a_send.at[0], a_recv.at[p], {"expert": expert}
                ).wait_recv()
            elif p % 2 == 0:
                for k in range(1, ny):
                    spread(k, y + ny - k).wait_recv()

    far_rows = pl.ds(2 * rows, rows)

    def spread(k, owner):
        ref = x_ref.at[far_rows, cols_of(owner % ny)]
        return remote(ref, ref, f_send.at[k - 1], f_recv.at[k - 1], {"dp": (y + k) % ny * nz + zl})

    def hand_on():
        for p in (4, 5):
            remote(
                out_ref.at[block(0), cols_of(y)],
                x_ref.at[block(p), cols_of(y)],
                a_send.at[0],
                a_recv.at[p],
                {"expert": expert},
            ).wait_recv()
        for k in range(1, ny):
            spread(k, y).start()
            sends.append(spread(k, y))

    def piece(j, d, h):
        return pl.ds(pl.multiple_of(j * rows + d * slots + h * part, part), part)

    lo, hi = pl.ds(0, half), pl.ds(half, half)

    def s1(j, d):
        return remote(s1_snd.at[j, d], s1_rcv.at[j, d], s1_send.at[j, d], s1_recv.at[j, d], pair[d])

    def s2(j, d):
        return remote(s2_snd.at[j, d], s2_rcv.at[j, d], s2_send.at[j, d], s2_recv.at[j, d], pair[1 - d])

    def g1(j, d, h):
        ref = d_ref.at[piece(j, d, h)]
        return remote(ref, ref, g1_send.at[j, d], g1_recv.at[j, d], pair[d])

    def stage0(j):
        wait_slabs(j)
        if j == 0:
            loads[0].wait()
            loads[1].wait()
        own = pl.ds(j * rows, rows)
        p_ref[own, :] = jnp.dot(x_ref[own, :], w_ref[...], preferred_element_type=F32)
        for d in range(2):
            s1_snd[j, d] = p_ref[piece(j, d, 1 - kept[d]), :].astype(BF16)
        for d in range(2):
            s1(j, d).start()
            sends.append(s1(j, d))

    def stage1(j):
        for d in range(2):
            mine = piece(j, d, kept[d])
            s1(j, d).wait_recv()
            both = p_ref[mine, :] + s1_rcv[j, d].astype(F32)
            p_ref[mine, :] = both
            s2_snd[j, d] = both.astype(BF16)
            s2(j, d).start()
            sends.append(s2(j, d))

    def stage2(j):
        if j == 0:
            loads[2].wait()
        for d in range(2):
            mine = piece(j, d, kept[d])
            hg_rows = pl.ds(pl.multiple_of(source(2 * j + d) * slots + kept[d] * part, part), part)
            upstream = hg_ref[hg_rows, :].astype(F32)
            s2(j, d).wait_recv()
            gate = p_ref[mine, lo] + s2_rcv[j, d, :, lo].astype(F32)
            upp = p_ref[mine, hi] + s2_rcv[j, d, :, hi].astype(F32)
            sg = jax.nn.sigmoid(gate)
            d_ref[mine, lo] = (upstream * upp * sg * (1.0 + gate * (1.0 - sg))).astype(BF16)
            d_ref[mine, hi] = (upstream * gate * sg).astype(BF16)
            g1(j, d, kept[d]).start()
            sends.append(g1(j, d, kept[d]))

    def stage4(j):
        for d in range(2):
            g1(j, d, 1 - kept[d]).wait_recv()
        own = pl.ds(j * rows, rows)
        rf_ref[own, :] = lax.dot_general(
            d_ref[own, :], w_ref[...], (((1,), (1,)), ((), ())), preferred_element_type=F32
        )
        r_ref[own, :] = rf_ref[own, :].astype(BF16)
        for k in range(1, ny):
            to = (y + k) % ny
            copy = remote(
                r_ref.at[own, cols_of(to)],
                yrcv.at[j, k - 1],
                y_send.at[j, k - 1],
                y_recv.at[j, k - 1],
                {"dp": to * nz + zl},
            )
            copy.start()
            sends.append(copy)

    def stage5(j):
        own = pl.ds(j * rows, rows)
        value = rf_ref[own, cols_of(y)]
        for k in range(1, ny):
            ref = yrcv.at[j, k - 1]
            remote(ref, ref, y_send.at[j, k - 1], y_recv.at[j, k - 1], {"dp": dp}).wait_recv()
            value = value + yrcv[j, k - 1].astype(F32)
        ysum[own, :] = value.astype(BF16)
        for p in (2 * j, 2 * j + 1):
            dx, c = slabs[p]
            if dx == 0:
                if p % 2:
                    continue
                p, to = 1 - core, x * 2 + 1 - core
            else:
                to = source(p)
            index = place((nx - dx) % nx, core)
            copy = remote(
                ysum.at[block(p)], ret_ref.at[block(expert)], r_send.at[p], r_recv.at[index], {"expert": to}
            )
            copy.start()
            sends.append(copy)
        if j == 0:
            ret_ref[block(expert), :] = ysum[block(core), :]

    if nx == 4:
        plan = (0, 0), (0, 1), "F", (0, 3), (1, 0), (0, 2), (1, 1), (1, 3), (1, 2), (2, 0), (2, 1), (2, 2), (2, 3), (4, 0), (4, 1), (4, 2), (5, 0), (5, 1), (4, 3), "V", (5, 2), (5, 3), "W"
    else:
        plan = (0, 0), (1, 0), (2, 0), (4, 0), "V", (5, 0), "W"
    step = min(256, width)
    early = width // step // 2

    def grads(i, carry):
        cols = pl.ds(pl.multiple_of(i * step, step), step)
        both = lax.dot_general(
            x_ref[:, cols], d_ref[...], (((0,), (0,)), ((), ())), preferred_element_type=F32
        ).astype(BF16)
        gg_ref[cols, :] = both[:, :half]
        ug_ref[cols, :] = both[:, half:]
        return carry

    stores = [
        pltpu.make_async_copy(gg_ref, gg_hbm, store_sem.at[0]),
        pltpu.make_async_copy(ug_ref, ug_hbm, store_sem.at[1]),
    ]
    stages = (stage0, stage1, stage2, None, stage4, stage5)
    for act in plan:
        if act == "F":
            hand_on()
        elif act == "V":
            lax.fori_loop(0, early, grads, 0)
        elif act == "W":
            lax.fori_loop(early, width // step, grads, 0)
            for store in stores:
                store.start()
        else:
            stages[act[0]](act[1])

    for p in range(len(slabs)):
        dx, c = slabs[p]
        if dx == 0:
            if p:
                continue
            index, e = 1 - core, x * 2 + 1 - core
        else:
            index, e = p, source(p)
        ref = ret_ref.at[block(e)]
        remote(ref, ref, r_send.at[0], r_recv.at[index], {"expert": expert}).wait_recv()
    sum_ref[...] = jnp.dot(table_ref[...], ret_ref[...], preferred_element_type=F32)
    zsnd[...] = sum_ref[...].astype(BF16)

    owners = z_send.shape[0]
    first = (nz - owners) // 2
    few = tokens // owners
    is_owner = (zl >= first) & (zl < first + owners)
    my_m = jnp.clip(zl - first, 0, owners - 1)

    def band(m):
        return pl.ds(pl.multiple_of(m * few, few), few)

    def z_out(q, m):
        rel = (zl + nz - (first + m)) % nz
        return remote(
            zsnd.at[band(m), pl.ds(q * span, span)],
            zrcv.at[rel, :, pl.ds(q * span, span)],
            z_send.at[m, q],
            z_recv.at[rel, q],
            {"dp": y * nz + first + m},
        )

    def h_out(q, k):
        ref = og_ref.at[band(my_m), cut_of(y, q)]
        return remote(ref, ref, h_send.at[k, q], h_recv.at[my_m, q], {"dp": y * nz + (zl + k) % nz})

    for q in range(cuts):
        for m in range(owners):
            pl.when(zl != first + m)(lambda q=q, m=m: z_out(q, m).start())

    @pl.when(is_owner)
    def _():
        for q in range(cuts):
            value = sum_ref[band(my_m), pl.ds(q * span, span)]
            for k in range(1, nz):
                ref = zrcv.at[k, :, pl.ds(q * span, span)]
                remote(ref, ref, z_send.at[0, q], z_recv.at[k, q], {"dp": dp}).wait_recv()
                value = value + zrcv[k, :, pl.ds(q * span, span)].astype(F32)
            og_ref[band(my_m), cut_of(y, q)] = value.astype(BF16)
            for k in range(1, nz):
                h_out(q, k).start()

    for q in range(cuts):
        for m in range(owners):

            @pl.when(zl != first + m)
            def _(q=q, m=m):
                ref = og_ref.at[band(m), cut_of(y, q)]
                remote(ref, ref, h_send.at[0, q], h_recv.at[m, q], {"dp": dp}).wait_recv()

        for k in range(1, ny):
            ref = og_ref.at[:, cut_of(y, q)]
            copy = remote(ref, ref, o_send.at[k - 1, q], o_recv.at[k - 1, q], {"dp": (y + k) % ny * nz + zl})
            copy.start()
            sends.append(copy)
    for q in range(cuts):
        for k in range(1, ny):
            ref = og_ref.at[:, cut_of((y + ny - k) % ny, q)]
            remote(ref, ref, o_send.at[k - 1, q], o_recv.at[k - 1, q], {"dp": dp}).wait_recv()
    tg_out[...] = og_ref[...]

    for copy in sends:
        copy.wait_send()
    for q in range(cuts):
        for m in range(owners):
            pl.when(zl != first + m)(lambda q=q, m=m: z_out(q, m).wait_send())

    @pl.when(is_owner)
    def _():
        for q in range(cuts):
            for k in range(1, nz):
                h_out(q, k).wait_send()

    for store in stores:
        store.wait()


def on_device(sizes, tokens, expert_ids, w_gate, w_up, hidden_grad):
    ny, nz, nx = sizes
    count, width = tokens.shape
    half = w_gate.shape[2]
    rows = hidden_grad.shape[1]
    chunks = nx
    part = rows // chunks // 4
    share = width // ny
    owners = min(4, nz)
    near = max(ny - 1, 1)
    cuts = 1
    scratch = [
        VMEM((count, rows), BF16),
        VMEM((width, 2 * half), BF16),
        VMEM((rows, half), BF16),
        VMEM((rows, width), BF16),
        VMEM((rows, width), BF16),
        VMEM((rows, 2 * half), F32),
        VMEM((rows, 2 * half), BF16),
        VMEM((rows, width), BF16),
        VMEM((rows, width), F32),
        VMEM((chunks, near, rows // chunks, share), BF16),
        VMEM((rows, share), BF16),
        VMEM((rows, share), BF16),
        VMEM((chunks, 2, part, 2 * half), BF16),
        VMEM((chunks, 2, part, 2 * half), BF16),
        VMEM((chunks, 2, part, 2 * half), BF16),
        VMEM((chunks, 2, part, 2 * half), BF16),
        VMEM((count, share), F32),
        VMEM((count, share), BF16),
        VMEM((nz, count // owners, share), BF16),
        VMEM((count, width), BF16),
        VMEM((width, half), BF16),
        VMEM((width, half), BF16),
        DMA((3,)),
        DMA((2,)),
        DMA((2 * nx,)),
        DMA((2 * nx,)),
        DMA((near,)),
        DMA((near,)),
    ]
    scratch += [DMA((chunks, 2)) for _ in range(6)]
    scratch += [
        DMA((2 * nx,)),
        DMA((2 * nx,)),
        DMA((chunks, near)),
        DMA((chunks, near)),
        DMA((owners, cuts)),
        DMA((nz, cuts)),
        DMA((nz, cuts)),
        DMA((owners, cuts)),
        DMA((near, cuts)),
        DMA((near, cuts)),
    ]
    vmem = pl.BlockSpec(memory_space=VMEM)
    hbm = pl.BlockSpec(memory_space=ANY)
    tokens_grad, gate_grad, up_grad = pl.pallas_call(
        functools.partial(kernel, sizes),
        out_shape=(
            jax.ShapeDtypeStruct((count, width), BF16),
            jax.ShapeDtypeStruct((width, half), BF16),
            jax.ShapeDtypeStruct((width, half), BF16),
        ),
        in_specs=[vmem, vmem, hbm, hbm, hbm],
        out_specs=(vmem, hbm, hbm),
        scratch_shapes=scratch,
        compiler_params=pltpu.CompilerParams(
            collective_id=0, has_side_effects=True, vmem_limit_bytes=60 * 1024 * 1024
        ),
    )(expert_ids.T, tokens, hidden_grad[0], w_gate[0], w_up[0])
    return tokens_grad, gate_grad[None], up_grad[None]


def solution(mesh):
    dp, experts = mesh.shape["dp"], mesh.shape["expert"]
    sizes = {32: (4, 8), 4: (2, 2), 2: (2, 1), 1: (1, 1)}[dp] + (experts // 2,)
    in_specs = (
        P("expert", "tensor"),
        P("expert", None),
        P("expert", "tensor", "dp"),
        P("expert", "tensor", "dp"),
        P("expert", None, "dp"),
    )
    out_specs = (P("expert", "tensor"), P("expert", "tensor", "dp"), P("expert", "tensor", "dp"))
    return jax.shard_map(
        functools.partial(on_device, sizes),
        mesh=mesh,
        in_specs=in_specs,
        out_specs=out_specs,
        check_vma=False,
    )
```

time: 126 us -> 103 us (0.82)
  Pallas kernels: 118 us -> 97.7 us
  local copies, waits for them, and re-layouts: 7.3 us -> 4.64 us
    pallas_call x1, Pallas kernels: 118 us -> 97.7 us  [on_device(): pl.pallas_call(functools.partial(kernel, sizes), out_shape=(jax.ShapeDtyp...]
    unnamed x14 -> x5, local copies, waits for them, and re-layouts: 7.3 us -> 4.64 us
where the time goes in v2:
time: 103 us
  Pallas kernels  97.7 us (95%)
  local copies, waits for them, and re-layouts  4.64 us (5%)
    pallas_call x1, Pallas kernels, on_device(): pl.pallas_call(functools.partial(kernel, sizes), out_shape=(jax.ShapeDtyp...  97.7 us
    unnamed x5, local copies, waits for them, and re-layouts  4.64 us

profile of v2, /device:TPU:1, one launch (start us, length us, event | category | flops | bytes accessed | tf_op | source)
XLA Modules:
  0.0 102.9 jit_solution(1406056243878503870)
XLA Ops:
  0.6 97.7 %shard_map.76 = (bf16[64,1536]{1,0:T(8,128)(2,1)}, bf16[1536,256]{1,0:T(8,128)(2,1)}, bf16[1536,256]{1,0:T(8,128)(2,1)}) custom-call(s32[2,64]{1,0:T(2,128)} %bitcast.11, bf16[64,1536]{1,0:T(8,128)(2,1)} %tok_ref.1, bf16[256,256]{1,0:T(8,128)(2,1)} %bitcast.10, bf16[1536,256]{1,0:T(8,128)(2,1)} %bitcast.6, bf16[1536,256]{1,0:T(8,128)(2,1)} %bitcast.7), custom_call_target="tpu_custom_call" | custom-call | tf_op jit(solution)/shard_map/pallas_call | solution.py:490
  98.3 1.6 %copy.11 = bf16[64,1536]{1,0:T(8,128)(2,1)} copy(bf16[64,1536]{1,0:T(8,128)(2,1)} %get-tuple-element.12) | data formatting | bytes 393216
  99.9 0.0 copy-start
  99.9 2.1 %copy.12 = bf16[1,1536,256]{2,1,0:T(8,128)(2,1)} copy(bf16[1,1536,256]{2,1,0:T(8,128)(2,1)} %bitcast.9) | data formatting | bytes 1572864
  102.1 0.0 copy-done
  102.1 0.9 copy.13
Async XLA Ops:
  99.9 2.1 %copy-start = (bf16[1536,256]{1,0:T(8,128)(2,1)S(1)}, bf16[1536,256]{1,0:T(8,128)(2,1)}, u32[]{:S(2)}) copy-start(bf16[1536,256]{1,0:T(8,128)(2,1)} %get-tuple-element.8) | copy-start | bytes 2359300

commit v3 on v2

--- a/solution.py
+++ b/solution.py
@@ -28,13 +28,14 @@
 def kernel(
     sizes,
     ids_ref,
-    tok_ref,
+    tok_hbm,
     hg_hbm,
     wg_hbm,
     wu_hbm,
     tg_out,
     gg_hbm,
     ug_hbm,
+    tok_ref,
     table_ref,
     w_ref,
     hg_ref,
@@ -127,6 +128,7 @@
         greeted += 1
 
     loads = [
+        pltpu.make_async_copy(tok_hbm, tok_ref, load_sem.at[3]),
         pltpu.make_async_copy(wg_hbm, w_ref.at[:, pl.ds(0, half)], load_sem.at[0]),
         pltpu.make_async_copy(wu_hbm, w_ref.at[:, pl.ds(half, half)], load_sem.at[1]),
         pltpu.make_async_copy(hg_hbm, hg_ref, load_sem.at[2]),
@@ -147,6 +149,7 @@
     )
     table = jnp.where(chosen & (before == (row % slots).astype(F32)), 1.0, 0.0)
     table_ref[...] = table.T.astype(BF16)
+    loads[0].wait()
     out_ref[...] = jnp.dot(table.astype(BF16), tok_ref[...], preferred_element_type=F32).astype(BF16)
 
     pl.semaphore_wait(barrier, greeted)
@@ -230,8 +233,8 @@
     def stage0(j):
         wait_slabs(j)
         if j == 0:
-            loads[0].wait()
             loads[1].wait()
+            loads[2].wait()
         own = pl.ds(j * rows, rows)
         p_ref[own, :] = jnp.dot(x_ref[own, :], w_ref[...], preferred_element_type=F32)
         for d in range(2):
@@ -252,7 +255,7 @@
 
     def stage2(j):
         if j == 0:
-            loads[2].wait()
+            loads[3].wait()
         for d in range(2):
             mine = piece(j, d, kept[d])
             hg_rows = pl.ds(pl.multiple_of(source(2 * j + d) * slots + kept[d] * part, part), part)
@@ -443,6 +446,7 @@
     near = max(ny - 1, 1)
     cuts = 1
     scratch = [
+        VMEM((count, width), BF16),
         VMEM((count, rows), BF16),
         VMEM((width, 2 * half), BF16),
         VMEM((rows, half), BF16),
@@ -465,7 +469,7 @@
         VMEM((count, width), BF16),
         VMEM((width, half), BF16),
         VMEM((width, half), BF16),
-        DMA((3,)),
+        DMA((4,)),
         DMA((2,)),
         DMA((2 * nx,)),
         DMA((2 * nx,)),
@@ -486,7 +490,8 @@
         DMA((near, cuts)),
     ]
     vmem = pl.BlockSpec(memory_space=VMEM)
-    hbm = pl.BlockSpec(memory_space=ANY)
+    hbm = pl.BlockSpec(memory_space=pltpu.HBM)
+    free = pl.BlockSpec(memory_space=ANY)
     tokens_grad, gate_grad, up_grad = pl.pallas_call(
         functools.partial(kernel, sizes),
         out_shape=(
@@ -494,13 +499,19 @@
             jax.ShapeDtypeStruct((width, half), BF16),
             jax.ShapeDtypeStruct((width, half), BF16),
         ),
-        in_specs=[vmem, vmem, hbm, hbm, hbm],
-        out_specs=(vmem, hbm, hbm),
+        in_specs=[vmem, hbm, hbm, hbm, hbm],
+        out_specs=(vmem, free, free),
         scratch_shapes=scratch,
         compiler_params=pltpu.CompilerParams(
-            collective_id=0, has_side_effects=True, vmem_limit_bytes=60 * 1024 * 1024
+            collective_id=0, has_side_effects=True, vmem_limit_bytes=32 * 1024 * 1024
         ),
-    )(expert_ids.T, tokens, hidden_grad[0], w_gate[0], w_up[0])
+    )(
+        expert_ids.T,
+        pltpu.with_memory_space_constraint(tokens, pltpu.HBM),
+        pltpu.with_memory_space_constraint(hidden_grad[0], pltpu.HBM),
+        pltpu.with_memory_space_constraint(w_gate[0], pltpu.HBM),
+        pltpu.with_memory_space_constraint(w_up[0], pltpu.HBM),
+    )
     return tokens_grad, gate_grad[None], up_grad[None]
 
 

time: 103 us -> 101 us (0.981)
  local copies, waits for them, and re-layouts: 4.64 us -> 3.11 us
  Pallas kernels: 97.7 us -> 96.6 us
    unnamed x5, local copies, waits for them, and re-layouts: 4.64 us -> 3.11 us
    pallas_call x1, Pallas kernels: 97.7 us -> 96.6 us  [on_device(): pl.pallas_call(functools.partial(kernel, sizes), out_shape=(jax.ShapeDtyp...]
where the time goes in v3:
time: 101 us; the launch traced here: 100 us
  Pallas kernels  96.6 us (96%)
  local copies, waits for them, and re-layouts  3.11 us (3%)
    pallas_call x1, Pallas kernels, on_device(): pl.pallas_call(functools.partial(kernel, sizes), out_shape=(jax.ShapeDtyp...  96.6 us
    unnamed x5, local copies, waits for them, and re-layouts  3.11 us

profile of v3, /device:TPU:1, one launch (start us, length us, event | category | flops | bytes accessed | tf_op | source)
XLA Modules:
  0.0 100.3 jit_solution(11444094183615993524)
XLA Ops:
  0.6 0.0 copy-start
  0.6 0.7 copy-done
  1.3 96.6 %shard_map.76 = (bf16[64,1536]{1,0:T(8,128)(2,1)S(1)}, bf16[1536,256]{1,0:T(8,128)(2,1)S(1)}, bf16[1536,256]{1,0:T(8,128)(2,1)S(1)}) custom-call(s32[2,64]{1,0:T(2,128)S(1)} %bitcast.8, bf16[64,1536]{1,0:T(8,128)(2,1)} %tok_hbm.1, bf16[256,256]{1,0:T(8,128)(2,1)} %bitcast.11, bf16[1536,256]{1,0:T(8,128)(2,1)} %bitcast.9, bf16[1536,256]{1,0:T(8,128)(2,1)} %bitcast.10), custom_call_target="tpu_custom_call" | custom-call | tf_op jit(solution)/shard_map/pallas_call | solution.py:495
  97.9 0.7 copy.11
  98.6 0.9 copy.12
  99.5 0.9 copy.13
Async XLA Ops:
  0.6 0.7 copy-start

commit v4 on v3

--- a/solution.py
+++ b/solution.py
@@ -158,22 +158,27 @@
         return pl.ds(pl.multiple_of(e * slots, slots), slots)
 
     sends = []
-    dxs = [0, 2, 1, 3] if nx == 4 else [0]
     flat = 0
-    for dx in dxs:
-        for c in range(2):
-            if dx == 0 and c == 1:
-                continue
-            other = 1 - core if dx == 0 else c
-            to = ((x + nx - dx) % nx) * 2 + other
-            slab = place(dx, core)
-            src, dst = out_ref.at[block(to)], x_ref.at[block(slab)]
-            if dx == 2:
-                src, dst = out_ref.at[block(to), cols_of(y)], x_ref.at[block(slab), cols_of(y)]
-            copy = remote(src, dst, a_send.at[flat], a_recv.at[slab], {"expert": to})
-            copy.start()
-            sends.append(copy)
-            flat += 1
+
+    def send_slab(back, other, slab, share_only=False):
+        nonlocal flat
+        to = ((x + nx - back) % nx) * 2 + other
+        src, dst = out_ref.at[block(to)], x_ref.at[block(slab)]
+        if share_only:
+            src, dst = out_ref.at[block(to), cols_of(y)], x_ref.at[block(slab), cols_of(y)]
+        copy = remote(src, dst, a_send.at[flat], a_recv.at[slab], {"expert": to})
+        copy.start()
+        sends.append(copy)
+        flat += 1
+
+    send_slab(0, 1 - core, place(0, core))
+    if nx == 4:
+        for other in range(2):
+            send_slab(1 + 2 * core, other, 2 + core)
+        for other in range(2):
+            send_slab(2, other, place(2, core), True)
+        for other in range(2):
+            send_slab(3 - 2 * core, other, 7 - core)
     x_ref[block(core), :] = out_ref[block(expert), :]
 
     def source(p):
@@ -442,7 +447,7 @@
     chunks = nx
     part = rows // chunks // 4
     share = width // ny
-    owners = min(4, nz)
+    owners = min(2, nz)
     near = max(ny - 1, 1)
     cuts = 1
     scratch = [

time: 101 us -> 99.6 us (0.986)
  Pallas kernels: 96.6 us -> 95 us
    pallas_call x1, Pallas kernels: 96.6 us -> 95 us  [on_device(): pl.pallas_call(functools.partial(kernel, sizes), out_shape=(jax.ShapeDtyp...]
where the time goes in v4:
time: 99.6 us; the launch traced here: 98.8 us
  Pallas kernels  95 us (95%)
  local copies, waits for them, and re-layouts  3.11 us (3%)
    pallas_call x1, Pallas kernels, on_device(): pl.pallas_call(functools.partial(kernel, sizes), out_shape=(jax.ShapeDtyp...  95 us
    unnamed x5, local copies, waits for them, and re-layouts  3.11 us

profile of v4, /device:TPU:1, one launch (start us, length us, event | category | flops | bytes accessed | tf_op | source)
XLA Modules:
  0.0 98.8 jit_solution(4334389465902862805)
XLA Ops:
  0.6 0.0 copy-start
  0.6 0.7 copy-done
  1.3 95.0 %shard_map.76 = (bf16[64,1536]{1,0:T(8,128)(2,1)S(1)}, bf16[1536,256]{1,0:T(8,128)(2,1)S(1)}, bf16[1536,256]{1,0:T(8,128)(2,1)S(1)}) custom-call(s32[2,64]{1,0:T(2,128)S(1)} %bitcast.8, bf16[64,1536]{1,0:T(8,128)(2,1)} %tok_hbm.1, bf16[256,256]{1,0:T(8,128)(2,1)} %bitcast.11, bf16[1536,256]{1,0:T(8,128)(2,1)} %bitcast.9, bf16[1536,256]{1,0:T(8,128)(2,1)} %bitcast.10), custom_call_target="tpu_custom_call" | custom-call | tf_op jit(solution)/shard_map/pallas_call | solution.py:500
  96.3 0.7 copy.11
  97.0 0.9 copy.12
  97.9 0.9 copy.13
Async XLA Ops:
  0.6 0.7 copy-start

commit v5 on v4

--- a/solution.py
+++ b/solution.py
@@ -320,7 +320,7 @@
             ret_ref[block(expert), :] = ysum[block(core), :]
 
     if nx == 4:
-        plan = (0, 0), (0, 1), "F", (0, 3), (1, 0), (0, 2), (1, 1), (1, 3), (1, 2), (2, 0), (2, 1), (2, 2), (2, 3), (4, 0), (4, 1), (4, 2), (5, 0), (5, 1), (4, 3), "V", (5, 2), (5, 3), "W"
+        plan = (0, 0), (0, 1), "F", (0, 3), (1, 0), (0, 2), (1, 1), (1, 3), (1, 2), (2, 0), (2, 1), (2, 2), (2, 3), (4, 0), (4, 1), (4, 2), (5, 0), (5, 1), (4, 3), (5, 2), "V", (5, 3), "W"
     else:
         plan = (0, 0), (1, 0), (2, 0), (4, 0), "V", (5, 0), "W"
     step = min(256, width)

time: 99.6 us -> 99.6 us (level)
  no operation moved by 1% of the time
where the time goes in v5:
time: 99.6 us; the launch traced here: 98.8 us
  Pallas kernels  95 us (95%)
  local copies, waits for them, and re-layouts  3.11 us (3%)
    pallas_call x1, Pallas kernels, on_device(): pl.pallas_call(functools.partial(kernel, sizes), out_shape=(jax.ShapeDtyp...  95 us
    unnamed x5, local copies, waits for them, and re-layouts  3.11 us

profile of v5, /device:TPU:1, one launch (start us, length us, event | category | flops | bytes accessed | tf_op | source)
XLA Modules:
  0.0 98.8 jit_solution(14416082974417415590)
XLA Ops:
  0.6 0.0 copy-start
  0.6 0.7 copy-done
  1.3 95.0 %shard_map.76 = (bf16[64,1536]{1,0:T(8,128)(2,1)S(1)}, bf16[1536,256]{1,0:T(8,128)(2,1)S(1)}, bf16[1536,256]{1,0:T(8,128)(2,1)S(1)}) custom-call(s32[2,64]{1,0:T(2,128)S(1)} %bitcast.8, bf16[64,1536]{1,0:T(8,128)(2,1)} %tok_hbm.1, bf16[256,256]{1,0:T(8,128)(2,1)} %bitcast.11, bf16[1536,256]{1,0:T(8,128)(2,1)} %bitcast.9, bf16[1536,256]{1,0:T(8,128)(2,1)} %bitcast.10), custom_call_target="tpu_custom_call" | custom-call | tf_op jit(solution)/shard_map/pallas_call | solution.py:500
  96.3 0.7 copy.11
  97.0 0.9 copy.12
  97.9 0.9 copy.13
Async XLA Ops:
  0.6 0.7 copy-start
